TPU v7x, 32 devices: a whole 2x2x4 slice. The times are simulated.
32 devices in a mesh: seq: 8 (over z, x), expert: 4 (over y, core).
Axes of the slice: x: 2, y: 2, z: 4, core: 2. Of those that a mesh axis runs over, the one named last changes fastest.
Arguments:
- query: bfloat16 [32, 8192], P('expert'), may hold values from -100 to 100
- cached_key_block: bfloat16 [32, 1024, 512], P('expert', 'seq'), may hold values from -5 to 5
- cached_value_block: bfloat16 [32, 1024, 512], P('expert', 'seq'), may hold values from -6 to 6
- fresh_token_key: bfloat16 [32, 512], P('expert'), may hold values from -6 to 6
- fresh_token_value: bfloat16 [32, 512], P('expert'), may hold values from -6 to 6
- lengths: int32 [32], P('expert'), may hold values from 2 to 1024, as said below
- residual_in: bfloat16 [32, 4096], P('expert'), may hold values from -6 to 6
- o_weight: bfloat16 [8192, 4096], P('seq'), may hold values from -0.0625 to 0.0625
- norm_gain: float32 [4096], replicated, may hold values from 0.1 to 1.9
- gate_logits: float32 [32, 8], replicated, may hold values from -6 to 6
- routes: int32 [32, 8], replicated, may hold values from 0 to 63, all different within a row; in each aligned block of 8 rows (0 to 7, 8 to 15, ...) at most 2 rows name the same one
- w_gate: bfloat16 [128, 4096, 768], P(('seq', 'expert')), may hold values from -0.09375 to 0.09375
- w_up: bfloat16 [128, 4096, 768], P(('seq', 'expert')), may hold values from -0.09375 to 0.09375
- w_down: bfloat16 [128, 768, 4096], P(('seq', 'expert')), may hold values from -0.15625 to 0.15625
Outputs:
- layer_out: bfloat16 [32, 4096], P('expert', 'seq')
Inputs may be any that keep to these rules, and one draw needn't show every extreme that they name: `lengths`: the first row of every aligned block of 8 rows has length 1024. `routes`: each row names 8 different experts. In every aligned block of 8 rows no expert is named by more than 2 rows, a bound that some block reaches.
All inputs are finite; a program needn't handle non-finite values.
Results may differ from a plain program's by a relative error of at most 0.0044.
Values may be sent and summed in bfloat16 or wider, within the bound.
A program may use at most 192 MiB of HBM per device.

v0:
```python
import math

import jax
import jax.numpy as jnp
from jax import lax
from jax.sharding import PartitionSpec as P

D = 4096
QUERY_HEADS = 64
KEY_VALUE_HEADS = 4
HEAD_SIZE = 128
EXPERTS = 64
TOP = 8
CAP = 2


def combined_all(value, axis, join):
    pieces = jax.tree.map(lambda part: lax.all_gather(part, axis), value)
    head = jax.tree.map(lambda part: part[0], pieces)
    tail = jax.tree.map(lambda part: part[1:], pieces)
    so_far, _ = lax.scan(lambda so_far, piece: (join(so_far, piece), None), head, tail)
    return so_far


def merge_parts(first, second):
    peak_first, total_first, sum_first = first
    peak_second, total_second, sum_second = second
    peak_new = jnp.maximum(peak_first, peak_second)
    scale_first = jnp.exp(peak_first - peak_new)
    scale_second = jnp.exp(peak_second - peak_new)
    return (
        peak_new,
        total_first * scale_first + total_second * scale_second,
        sum_first * scale_first[..., None] + sum_second * scale_second[..., None],
    )


def slot_tables(route_rows, gate_rows, first_expert, count, capacity):
    owned_ids = first_expert + jnp.arange(count, dtype=jnp.int32)
    matches = route_rows[:, :, :, None] == owned_ids[None, None, None, :]
    hit_rows = jnp.any(matches, axis=2).astype(jnp.int32)
    weight = jnp.sum(jnp.where(matches, gate_rows[:, :, :, None], 0.0), axis=2)
    before = jnp.cumsum(hit_rows, axis=1) - hit_rows
    slot_ids = jnp.arange(capacity, dtype=jnp.int32)
    chosen_experts = (hit_rows[..., None] == 1) & (before[..., None] == slot_ids)
    placed = jnp.transpose(chosen_experts, (0, 2, 3, 1))
    shares = jnp.where(placed, jnp.transpose(weight, (0, 2, 1))[:, :, None, :], 0.0)
    return (placed, shares)


def on_device(
    query,
    cached_key_block,
    cached_value_block,
    fresh_token_key,
    fresh_token_value,
    lengths,
    residual_in,
    o_weight,
    norm_gain,
    gate_logits,
    routes,
    w_gate,
    w_up,
    w_down,
):
    highest_score = lax.Precision.HIGHEST
    local_row_count = query.shape[0]
    position_span = cached_key_block.shape[1]
    query_group = QUERY_HEADS // KEY_VALUE_HEADS
    seq_count = lax.axis_size("seq")
    seq_pos = lax.axis_index("seq")
    grp_count = lax.axis_size("expert")
    grp_pos = lax.axis_index("expert")
    softmax_scale = 1.0 / math.sqrt(HEAD_SIZE)
    heads_dev = QUERY_HEADS // seq_count
    query_rows = query.reshape(local_row_count, KEY_VALUE_HEADS, query_group, HEAD_SIZE)
    local_keys = cached_key_block.reshape(
        local_row_count, position_span, KEY_VALUE_HEADS, HEAD_SIZE
    )
    local_values = cached_value_block.reshape(
        local_row_count, position_span, KEY_VALUE_HEADS, HEAD_SIZE
    ).astype(jnp.float32)
    scores = (
        jnp.einsum("rkgd,rpkd->rkgp", query_rows, local_keys, preferred_element_type=jnp.float32)
        * softmax_scale
    )
    positions = seq_pos * position_span + jnp.arange(position_span, dtype=jnp.int32)
    valid = (positions[None, :] < lengths[:, None])[:, None, None, :]
    masked = jnp.where(valid, scores, -1e30)
    peak_loc = jnp.max(masked, axis=-1)
    weights = jnp.where(valid, jnp.exp(masked - peak_loc[..., None]), 0.0)
    total_loc = jnp.sum(weights, axis=-1).reshape(local_row_count, QUERY_HEADS)
    summed_output = jnp.einsum(
        "rkgp,rpkd->rkgd", weights, local_values, precision=highest_score
    ).reshape(local_row_count, QUERY_HEADS, HEAD_SIZE)
    peak_loc = peak_loc.reshape(local_row_count, QUERY_HEADS)
    self_token_score = (
        jnp.einsum(
            "sznj,szj->szn",
            query_rows,
            fresh_token_key.reshape(local_row_count, KEY_VALUE_HEADS, HEAD_SIZE),
            preferred_element_type=jnp.float32,
        )
        * softmax_scale
    ).reshape(local_row_count, QUERY_HEADS)
    own_value = (
        jnp.broadcast_to(
            fresh_token_value.reshape(local_row_count, KEY_VALUE_HEADS, 1, HEAD_SIZE),
            (local_row_count, KEY_VALUE_HEADS, query_group, HEAD_SIZE),
        )
        .reshape(local_row_count, QUERY_HEADS, HEAD_SIZE)
        .astype(jnp.float32)
    )
    own_score_dev = lax.dynamic_slice_in_dim(self_token_score, seq_pos * heads_dev, heads_dev, 1)
    own_value_dev = lax.dynamic_slice_in_dim(own_value, seq_pos * heads_dev, heads_dev, 1)
    peak_all, total_all, summed_all = combined_all(
        (peak_loc, total_loc, summed_output), "seq", merge_parts
    )
    peak_dev = lax.dynamic_slice_in_dim(peak_all, seq_pos * heads_dev, heads_dev, 1)
    total_dev = lax.dynamic_slice_in_dim(total_all, seq_pos * heads_dev, heads_dev, 1)
    summed_dev = lax.dynamic_slice_in_dim(summed_all, seq_pos * heads_dev, heads_dev, 1)
    top_dev = jnp.maximum(peak_dev, own_score_dev)
    factor = jnp.exp(peak_dev - top_dev)
    total_dev = total_dev * factor
    summed_dev = summed_dev * factor[..., None]
    self_token_weight = jnp.exp(own_score_dev - top_dev)
    total_dev = total_dev + self_token_weight
    summed_dev = summed_dev + self_token_weight[..., None] * own_value_dev
    attended = (
        (summed_dev / total_dev[..., None])
        .astype(jnp.bfloat16)
        .reshape(local_row_count, heads_dev * HEAD_SIZE)
    )
    projected_part = jnp.dot(attended, o_weight, preferred_element_type=jnp.float32)
    projected = lax.psum(projected_part, "seq")
    stream = residual_in.astype(jnp.float32) + projected
    normed = (
        stream * lax.rsqrt(jnp.mean(stream * stream, axis=-1, keepdims=True) + 1e-06) * norm_gain
    ).astype(jnp.bfloat16)
    gates = jax.nn.softmax(gate_logits, axis=-1)
    exp_dev = EXPERTS // seq_count
    pieces_dev = w_gate.shape[0]
    route_rows = routes.reshape(grp_count, local_row_count, TOP)
    gate_rows = gates.reshape(grp_count, local_row_count, TOP)
    placed, shares = slot_tables(route_rows, gate_rows, seq_pos * exp_dev, exp_dev, CAP)
    own_placed = lax.dynamic_slice_in_dim(placed, grp_pos, 1, 0).astype(jnp.bfloat16)
    outgoing = jnp.einsum(
        "gjcr,rd->gjcd", own_placed, normed, preferred_element_type=jnp.float32
    ).astype(jnp.bfloat16)
    local_ids = (grp_pos * pieces_dev + jnp.arange(pieces_dev, dtype=jnp.int32)) // 2
    select = local_ids[:, None] == jnp.arange(exp_dev, dtype=jnp.int32)[None, :]
    select_rows = select.astype(jnp.bfloat16)
    select_back = select.astype(jnp.float32)
    rows_in = jnp.einsum(
        "njcd,pj->npcd",
        lax.all_gather(outgoing, "expert", axis=0, tiled=True),
        select_rows,
        preferred_element_type=jnp.float32,
    ).astype(jnp.bfloat16)
    gate_act = jnp.einsum("npcd,pdf->npcf", rows_in, w_gate, preferred_element_type=jnp.float32)
    up_act = jnp.einsum("npcd,pdf->npcf", rows_in, w_up, preferred_element_type=jnp.float32)
    hidden = (jax.nn.silu(gate_act) * up_act).astype(jnp.bfloat16)
    result = jnp.einsum("npcf,pfd->npcd", hidden, w_down, preferred_element_type=jnp.float32)
    partial_out = jnp.einsum("npcd,pj->njcd", result, select_back, precision=highest_score)
    width_dev = D // seq_count
    split_out = partial_out.reshape(grp_count, exp_dev, CAP, seq_count, width_dev)
    contrib = jnp.einsum("gjcr,gjcsd->sgrd", shares, split_out, precision=highest_score).reshape(
        seq_count * grp_count * local_row_count, width_dev
    )
    added = lax.psum_scatter(contrib, ("seq", "expert"), scatter_dimension=0, tiled=True)
    stream_cols = lax.dynamic_slice_in_dim(stream, seq_pos * width_dev, width_dev, 1)
    return (stream_cols + added).astype(jnp.bfloat16)


def solution(mesh):
    placed = (
        P("expert", None),
        P("expert", "seq", None),
        P("expert", "seq", None),
        P("expert", None),
        P("expert", None),
        P("expert"),
        P("expert", None),
        P("seq", None),
        P(),
        P(),
        P(),
        P(("seq", "expert"), None, None),
        P(("seq", "expert"), None, None),
        P(("seq", "expert"), None, None),
    )
    return jax.shard_map(
        on_device, mesh=mesh, in_specs=placed, out_specs=P("expert", "seq"), check_vma=False
    )
```

profile of v0, /device:TPU:0, one launch (start us, length us, event | category | flops | bytes accessed | tf_op | source)
XLA Modules:
  0.0 346.3 jit_solution(2211389372781068628)
XLA Ops:
  6.5 0.0 copy-start
  6.5 0.0 copy-start.2
  6.5 0.0 copy-start.3
  6.5 0.0 all-gather.3.cloned.1.call-start
  6.6 0.8 broadcast_compare_fusion
  7.4 0.4 copy-done
  7.8 1.6 fusion.81
  9.4 3.0 fusion.26
  12.4 0.0 all-gather.3.cloned.1.call-update
  12.4 0.0 all-reduce.2.cloned.1.call-start
  12.4 0.1 all_gather_reshape.9
  12.5 0.3 fusion.34
  12.8 0.1 all_gather_reshape.10
  12.9 32.3 %all_gather.12 = f32[8,8,64]{2,1,0:T(8,128)S(1)} all-gather(f32[1,8,64]{2,1,0:T(8,128)S(1)} %all_gather_reshape.9), channel_id=1, replica_groups=mesh['seq'=8,'expert'=4] {'seq'}, dimensions={0}, use_global_device_ids=true | all-gather | bytes 18432 | tf_op jit(solution)/shard_map/all_gather | solution.py:18
  45.2 30.7 %all_gather.13 = f32[8,8,64]{2,1,0:T(8,128)S(1)} all-gather(f32[1,8,64]{2,1,0:T(8,128)S(1)} %all_gather_reshape.10), channel_id=1, replica_groups=mesh['seq'=8,'expert'=4] {'seq'}, dimensions={0}, use_global_device_ids=true | all-gather | bytes 18432 | tf_op jit(solution)/shard_map/all_gather | solution.py:18
  75.9 1.1 fusion.41
  77.0 0.1 reshape.125
  77.1 0.7 bitcast_convert_fusion
  77.8 0.8 copy.61
  78.5 0.1 compare_reduce_fusion
  78.7 0.1 copy.45
  78.8 0.1 copy.44
  78.9 0.7 reduce_max.19
  79.6 0.7 fusion.69
  80.3 0.7 fusion.68
  81.0 0.0 all-gather.3.cloned.1.call-done
  81.0 1.0 slice_bitcast_fusion
  82.0 1.6 slice.29
  83.6 2.1 while.14
  83.7 0.3 fusion.91
  84.0 0.3 fusion.91
  84.3 0.3 fusion.91
  84.6 0.3 fusion.91
  84.9 0.3 fusion.91
  85.2 0.3 fusion.91
  85.5 0.3 fusion.91
  85.7 0.1 multiply_add_fusion
  85.8 0.1 fusion.60
  85.9 5.2 %fusion.52 = f32[8,4096]{1,0:T(8,128)} fusion(bf16[1024,4096]{1,0:T(8,128)(2,1)} %param.23, bf16[1,8,8,128]{3,2,1,0:T(8,128)(2,1)S(1)} %fusion.60), kind=kOutput, calls=%fused_computation.59 | convolution fusion | flops 67108864 | bytes 8536064 | tf_op jit(solution)/shard_map/dot_general | solution.py:135
  91.2 0.0 all-reduce.2.cloned.1.call-update
  91.2 0.0 reduce-scatter.2.cloned.1.call-start
  91.3 0.1 copy.62
  91.4 0.1 fusion.37
  91.5 70.4 %all-reduce.2.cloned.1.call-done = f32[8,4096]{1,0:T(8,128)} async-done(((f32[8,4096]{1,0:T(8,128)}), f32[8,4096]{1,0:T(8,128)}) %all-reduce.2.cloned.1.call-update) | async-done | bytes 131088 | tf_op jit(solution)/shard_map/psum | solution.py:136
  162.0 0.0 copy-done.2
  162.0 1.1 multiply_reduce_fusion
  163.0 0.0 copy-done.3
  163.0 0.2 convolution_convert_fusion.1
  163.3 7.3 %all-gather = bf16[32,2,4096]{2,0,1:T(8,128)(2,1)S(1)} all-gather(bf16[8,2,4096]{2,0,1:T(8,128)(2,1)S(1)} %convolution_convert_fusion.1), channel_id=2, replica_groups=mesh['seq'=8,'expert'=4] {'expert'}, dimensions={0}, use_global_device_ids=true | all-gather | bytes 655360 | tf_op jit(solution)/shard_map/all_gather | solution.py:157
  170.6 0.4 fusion.12
  171.0 0.0 copy-start.1
  171.0 10.2 %fusion.14 = f32[4,4,2,768]{3,0,2,1:T(4,128)S(1)} fusion(bf16[4,4096,768]{2,1,0:T(8,128)(2,1)} %param.27, bf16[4,4,2,4096]{3,1,2,0:T(4,128)(2,1)S(1)} %fusion.12), kind=kOutput, calls=%fused_computation.21 | convolution fusion | flops 201326592 | bytes 25526272 | tf_op jit(solution)/shard_map/npcd,pdf->npcf/dot_general | solution.py:161
  181.2 10.2 %fusion.23 = bf16[4,4,2,768]{3,0,2,1:T(4,128)(2,1)S(1)} fusion(bf16[4,4096,768]{2,1,0:T(8,128)(2,1)} %param.28, bf16[4,4,2,4096]{3,1,2,0:T(4,128)(2,1)S(1)} %fusion.12, f32[4,4,2,768]{3,0,2,1:T(4,128)S(1)} %fusion.14), kind=kOutput, calls=%fused_computation.24 | convolution fusion | flops 201474048 | bytes 25575424 | tf_op jit(solution)/shard_map/npcd,pdf->npcf/dot_general | solution.py:162
  191.4 11.7 %fusion.9 = f32[4,4,2,4096]{3,0,2,1:T(4,128)S(1)} fusion(bf16[4,4,2,768]{3,0,2,1:T(4,128)(2,1)S(1)} %fusion.23, bf16[4,768,4096]{2,1,0:T(8,128)(2,1)} %param.29), kind=kOutput, calls=%fused_computation.14 | convolution fusion | flops 201326592 | bytes 25739264 | tf_op jit(solution)/shard_map/npcf,pfd->npcd/dot_general | solution.py:164
  203.1 1.0 fusion.31
  204.1 0.7 convolution_bitcast_fusion
  204.8 0.8 copy.52
  205.6 0.0 reduce-scatter.2.cloned.1.call-update
  205.7 132.8 %reduce-scatter.2.cloned.1.call-done = f32[8,512]{1,0:T(8,128)} async-done(((f32[256,512]{1,0:T(8,128)}), f32[8,512]{1,0:T(8,128)}) %reduce-scatter.2.cloned.1.call-update) | async-done | bytes 16400 | tf_op jit(solution)/shard_map/reduce_scatter | solution.py:171
  338.5 1.3 add_convert_fusion
  339.8 0.0 copy-done.1
  (23 shorter events, 0.2 us)
Async XLA Ops:
  6.5 1.2 copy-start
  6.5 155.4 %copy-start.2 = (bf16[8,4096]{1,0:T(8,128)(2,1)S(1)}, bf16[8,4096]{1,0:T(8,128)(2,1)}, u32[]{:S(2)}) copy-start(bf16[8,4096]{1,0:T(8,128)(2,1)} %param.22) | copy-start | bytes 196612
  6.5 156.5 %copy-start.3 = (f32[4096]{0:T(1024)S(1)}, f32[4096]{0:T(1024)}, u32[]{:S(2)}) copy-start(f32[4096]{0:T(1024)} %param.24) | copy-start | bytes 49156
  6.5 74.5 %all-gather.3.cloned.1.call-start = ((), (), s32[]{:S(2)}) async-start(), calls=%async_computation.1 | async-start | bytes 2359296 | tf_op jit(solution)/shard_map/all_gather | solution.py:18
  12.4 149.6 %all-reduce.2.cloned.1.call-start = ((), (), s32[]{:S(2)}) async-start(), calls=%async_computation.2 | async-start | bytes 262144 | tf_op jit(solution)/shard_map/psum | solution.py:136
  91.2 247.2 %reduce-scatter.2.cloned.1.call-start = ((), (), s32[]{:S(2)}) async-start(), calls=%async_computation.3 | async-start | bytes 540672 | tf_op jit(solution)/shard_map/reduce_scatter | solution.py:171
  171.0 168.8 %copy-start.1 = (bf16[8,128,512]{2,1,0:T(8,128)(2,1)S(1)}, bf16[8,128,512]{2,1,0:T(8,128)(2,1)}, u32[]{:S(2)}) copy-start(bf16[8,128,512]{2,1,0:T(8,128)(2,1)} %param.17) | copy-start | bytes 3145732
Sparse Core Ops, SparseCore 0:
  12.5 52.3 all-gather.2
  91.3 70.5 all-reduce.1
  205.8 132.6 reduce-scatter.1
where the time goes:
time: 347 us; the launch traced here: 346 us
  waiting for transfers between devices  203 us (59%)
  blocking collectives  70.3 us (20%)
  matrix products  45.3 us (13%)
  between operations  13.3 us (4%)
  other arithmetic  8.75 us (3%)
  local copies, waits for them, and re-layouts  5.11 us (1%)
    reduce_scatter x1, waiting for transfers between devices, on_device(): lax.psum_scatter(contrib, ('seq', 'expert'), scatter_dimension=0, tiled=T...  133 us
    psum x1, waiting for transfers between devices, on_device(): projected = lax.psum(projected_part, 'seq')  70.4 us
    all_gather x2, blocking collectives, combined_all(): pieces = jax.tree.map(lambda part: lax.all_gather(part, axis), value)  63 us
    dot_general x1, matrix products, on_device(): jnp.einsum('npcf,pfd->npcd', hidden, w_down, preferred_element_type=jnp.f...  11.7 us
    dot_general x1, matrix products, on_device(): jnp.einsum('npcd,pdf->npcf', rows_in, w_gate, preferred_element_type=jnp....  10.2 us
    dot_general x1, matrix products, on_device(): jnp.einsum('npcd,pdf->npcf', rows_in, w_up, preferred_element_type=jnp.fl...  10.2 us
    all_gather x1, blocking collectives, on_device(): lax.all_gather(outgoing, 'expert', axis=0, tiled=True)  7.34 us
  transfers between devices with their start and end apart: 3, of which 2 were waited for; matrix products, arithmetic and copies ran while one was open for 2% of the time, Pallas kernels for 0%

commit v1 on v0

v1 whole, which is shorter than its diff:
```python
import functools
import math

import jax
import jax.numpy as jnp
from jax import lax
from jax.experimental import pallas as pl
from jax.experimental.pallas import tpu as pltpu
from jax.sharding import PartitionSpec as P

KEY_VALUE_HEADS = 4
HEAD_SIZE = 128
MESH = pl.DeviceIdType.MESH
UP_SLOTS = 8
DOWN_SLOTS = 2
BF = jnp.bfloat16
F32 = jnp.float32


def layer_kernel(
    S, E, R, HEADS, D, FH, PIECES, NA, NB,
    len_ref, q_ref, fk_ref, fv_ref, res_ref, gain_ref, logit_ref, route_ref,
    k_hbm, v_hbm, ow_hbm, wg_hbm, wu_hbm, wd_hbm,
    out_ref,
    kbuf, vbuf, owbuf, abuf, bbuf,
    sbuf1, rbuf1, att, sbuf2, rbuf2, strm, xsend, xg, xs, acc, cbuf, rc,
    kv_sem, ow_sem, a_sem, b_sem,
    ss1, rs1, ss2, rs2, ss3, rs3, ss4, rs4,
):
    N = S * E
    T = E * R
    W = D // S
    HD = HEADS // S
    KVH = KEY_VALUE_HEADS
    HS = HEAD_SIZE
    GROUP = HEADS // KVH
    SPAN = kbuf.shape[1]
    HALF = D // 2
    TA = PIECES * 4
    seq = lax.axis_index("seq")
    exp = lax.axis_index("expert")
    me = seq * E + exp

    barrier = pltpu.get_barrier_semaphore()

    def greet(j, _):
        t = lax.rem(me + j, N)
        pl.semaphore_signal(
            barrier, inc=1, device_id={"seq": t // E, "expert": lax.rem(t, E)}, device_id_type=MESH
        )
        return 0

    lax.fori_loop(1, N, greet, 0)

    k_copy = pltpu.make_async_copy(k_hbm, kbuf, kv_sem.at[0])
    v_copy = pltpu.make_async_copy(v_hbm, vbuf, kv_sem.at[1])
    ow_copy = pltpu.make_async_copy(ow_hbm, owbuf, ow_sem.at[0])

    def a_copy(p, i, slot):
        src = wg_hbm if i % 2 == 0 else wu_hbm
        return pltpu.make_async_copy(
            src.at[p, pl.ds((i // 2) * HALF, HALF), :], abuf.at[slot], a_sem.at[slot]
        )

    def b_copy(p, slot):
        return pltpu.make_async_copy(wd_hbm.at[p], bbuf.at[slot], b_sem.at[slot])

    k_copy.start()
    v_copy.start()
    ow_copy.start()
    for p in range(PIECES):
        for i in range(4):
            if p * 4 + i < NA:
                a_copy(p, i, p * 4 + i).start()
        if p < NB:
            b_copy(p, p).start()

    scale = 1.0 / math.sqrt(HS)
    head_row = lax.broadcasted_iota(jnp.int32, (HEADS, KVH * HS), 0) // GROUP
    head_col = lax.broadcasted_iota(jnp.int32, (HEADS, KVH * HS), 1) // HS
    diag = head_row == head_col
    position = seq * SPAN + lax.broadcasted_iota(jnp.int32, (HEADS, SPAN), 1)
    lane = lax.broadcasted_iota(jnp.int32, (HEADS, HS), 1)
    has_own = seq == 0

    def spread(row):
        return jnp.concatenate(
            [jnp.broadcast_to(row[:, k * HS : (k + 1) * HS], (GROUP, HS)) for k in range(KVH)], axis=0
        )

    k_copy.wait()
    scores = []
    for r in range(R):
        q = q_ref[r]
        wide = jnp.where(diag, jnp.concatenate([q] * KVH, axis=1), jnp.zeros((), BF))
        scores.append(
            lax.dot_general(wide, kbuf[r], (((1,), (1,)), ((), ())), preferred_element_type=F32) * scale
        )
    v_copy.wait()
    fk = fk_ref[...].astype(F32)
    fv = fv_ref[...].astype(F32)
    packed = jnp.zeros((HEADS, HS), F32)
    for r in range(R):
        valid = position < len_ref[r]
        masked = jnp.where(valid, scores[r], -1e30)
        own = jnp.sum(q_ref[r].astype(F32) * spread(fk[r : r + 1]), axis=1, keepdims=True) * scale
        own = jnp.where(has_own, own, -1e30)
        peak = jnp.maximum(jnp.max(masked, axis=1, keepdims=True), own)
        weight = jnp.where(valid, jnp.exp(masked - peak), 0.0)
        own_weight = jnp.where(has_own, jnp.exp(own - peak), 0.0)
        total = jnp.sum(weight, axis=1, keepdims=True) + own_weight
        high = weight.astype(BF)
        low = (weight - high.astype(F32)).astype(BF)
        both = jnp.dot(jnp.concatenate([high, low], axis=0), vbuf[r], preferred_element_type=F32)
        both = both[:HEADS] + both[HEADS:]
        summed = jnp.concatenate(
            [both[k * GROUP : (k + 1) * GROUP, k * HS : (k + 1) * HS] for k in range(KVH)], axis=0
        )
        summed = summed + own_weight * spread(fv[r : r + 1])
        packed = jnp.where(lane == r, peak, jnp.where(lane == R + r, total, packed))
        for s in range(S):
            sbuf1[s, r] = summed[s * HD : (s + 1) * HD]
    for s in range(S):
        sbuf1[s, R] = packed[s * HD : (s + 1) * HD]

    pl.semaphore_wait(barrier, N - 1)

    def copy1(j):
        peer = lax.rem(seq + j, S)
        return pltpu.make_async_remote_copy(
            src_ref=sbuf1.at[peer], dst_ref=rbuf1.at[j], send_sem=ss1.at[j], recv_sem=rs1.at[j],
            device_id={"seq": peer, "expert": exp}, device_id_type=MESH,
        )

    def start1(j, _):
        copy1(j).start()
        return 0

    def wait1(j, _):
        copy1(j).wait_recv()
        return 0

    lax.fori_loop(1, S, start1, 0)
    rbuf1[0] = sbuf1[seq]
    lax.fori_loop(1, S, wait1, 0)

    stats = rbuf1[:, R]
    for r in range(R):
        peak = stats[:, :, r : r + 1]
        total = stats[:, :, R + r : R + r + 1]
        factor = jnp.exp(peak - jnp.max(peak, axis=0, keepdims=True))
        att[r] = jnp.sum(factor * rbuf1[:, r], axis=0) / jnp.sum(factor * total, axis=0)
    attended = jnp.concatenate([att[:, h, :] for h in range(HD)], axis=1).astype(BF)

    ow_copy.wait()

    def copy2(j):
        peer = lax.rem(seq + j, S)
        return pltpu.make_async_remote_copy(
            src_ref=sbuf2.at[j], dst_ref=rbuf2.at[j], send_sem=ss2.at[j], recv_sem=rs2.at[j],
            device_id={"seq": peer, "expert": exp}, device_id_type=MESH,
        )

    def project(j):
        cols = pl.ds(pl.multiple_of(lax.rem(seq + j, S) * W, W), W)
        return jnp.dot(attended, owbuf[:, cols], preferred_element_type=F32)

    def start2(j, _):
        sbuf2[j] = project(j)
        copy2(j).start()
        return 0

    def wait2(j, _):
        copy2(j).wait_recv()
        return 0

    lax.fori_loop(1, S, start2, 0)
    rbuf2[0] = project(0)
    lax.fori_loop(1, S, wait2, 0)

    own_cols = pl.ds(pl.multiple_of(seq * W, W), W)
    stream = res_ref[:, own_cols].astype(F32) + jnp.sum(rbuf2[...], axis=0)
    strm[...] = stream
    squares = jnp.sum(stream * stream, axis=1, keepdims=True)
    part0 = squares.astype(BF).astype(F32)
    part1 = (squares - part0).astype(BF).astype(F32)
    part2 = squares - part0 - part1
    lane_r = lax.broadcasted_iota(jnp.int32, (R, 128), 1)
    tail = jnp.where(
        lane_r == 0, part0, jnp.where(lane_r == 1, part1, jnp.where(lane_r == 2, part2, 0.0))
    )
    xsend[...] = jnp.concatenate([stream * gain_ref[:, own_cols], tail], axis=1).astype(BF)

    def target(j):
        t = lax.rem(me + j, N)
        return t // E, lax.rem(t, E)

    def copy3(j, dst):
        ts, te = target(j)
        return pltpu.make_async_remote_copy(
            src_ref=xsend, dst_ref=dst, send_sem=ss3.at[j], recv_sem=rs3.at[j],
            device_id={"seq": ts, "expert": te}, device_id_type=MESH,
        )

    def start3(j, _):
        copy3(j, xg.at[seq, exp]).start()
        return 0

    def wait3(j, _):
        ts, te = target(N - j)
        copy3(j, xg.at[ts, te]).wait_recv()
        return 0

    lax.fori_loop(1, N, start3, 0)
    xg[seq, exp] = xsend[...]

    logits = logit_ref[...]
    odds = jnp.exp(logits - jnp.max(logits, axis=1, keepdims=True))
    gates = odds / jnp.sum(odds, axis=1, keepdims=True)

    lax.fori_loop(1, N, wait3, 0)
    squares = jnp.zeros((T, 1), F32)
    for s in range(S):
        block = xg[s].astype(F32).reshape(T, W + 128)
        xs[(s * W) // HALF, :, (s * W) % HALF : (s * W) % HALF + W] = block[:, :W].astype(BF)
        squares = squares + jnp.sum(block[:, W:], axis=1, keepdims=True)
    inverse = lax.rsqrt(squares * (1.0 / D) + 1e-6)

    def copy4(c, e):
        return pltpu.make_async_remote_copy(
            src_ref=cbuf.at[c, e], dst_ref=rc.at[me], send_sem=ss4.at[c * E + e], recv_sem=rs4.at[me],
            device_id={"seq": c, "expert": e}, device_id_type=MESH,
        )

    def piece(p, _):
        acts = []
        for half in range(2):
            for m in range(2):
                i = half * 2 + m
                unit = p * 4 + i
                slot = lax.rem(unit, NA)
                a_copy(p, i, slot).wait()
                part = jnp.dot(xs[half], abuf[slot], preferred_element_type=F32)
                if half == 0:
                    acts.append(part)
                else:
                    acts[m] = acts[m] + part
                if TA > NA:

                    @pl.when(unit + NA < TA)
                    def _():
                        a_copy(p + NA // 4, i, slot).start()

        gate_act = acts[0] * inverse
        up_act = acts[1] * inverse
        hidden = (gate_act / (1.0 + jnp.exp(-gate_act)) * up_act).astype(BF)
        expert_id = (me * PIECES + p) // 2
        coeff = jnp.sum(jnp.where(route_ref[...] == expert_id, gates, 0.0), axis=1, keepdims=True)
        slot = lax.rem(p, NB)
        b_copy(p, slot).wait()

        def columns(j, _):
            c = lax.rem(seq + j, S)
            cols = pl.ds(pl.multiple_of(c * W, W), W)
            result = coeff * jnp.dot(hidden, bbuf[slot, :, cols], preferred_element_type=F32)

            @pl.when(p == 0)
            def _():
                acc[c] = result

            @pl.when(p > 0)
            def _():
                acc[c] = acc[c] + result

            @pl.when(p == PIECES - 1)
            def _():
                value = acc[c]
                for e in range(E):
                    cbuf[c, e] = value[e * R : (e + 1) * R].astype(BF)

                    @pl.when(c * E + e != me)
                    def _():
                        copy4(c, e).start()

            return 0

        lax.fori_loop(1, S + 1, columns, 0)
        if PIECES > NB:

            @pl.when(p + NB < PIECES)
            def _():
                b_copy(p + NB, slot).start()

        return 0

    lax.fori_loop(0, PIECES, piece, 0)
    rc[me] = cbuf[seq, exp]

    def wait4(j, _):
        ts, te = target(j)
        src = ts * E + te
        pltpu.make_async_remote_copy(
            src_ref=cbuf.at[ts, te], dst_ref=rc.at[src], send_sem=ss4.at[src], recv_sem=rs4.at[src],
            device_id={"seq": ts, "expert": te}, device_id_type=MESH,
        ).wait_recv()
        return 0

    lax.fori_loop(1, N, wait4, 0)
    out_ref[...] = (strm[...] + jnp.sum(rc[...].astype(F32), axis=0)).astype(BF)

    def sent12(j, _):
        copy1(j).wait_send()
        copy2(j).wait_send()
        return 0

    def sent34(j, _):
        copy3(j, xg.at[seq, exp]).wait_send()
        ts, te = target(j)
        copy4(ts, te).wait_send()
        return 0

    lax.fori_loop(1, S, sent12, 0)
    lax.fori_loop(1, N, sent34, 0)


def on_device(
    query, cached_key_block, cached_value_block, fresh_token_key, fresh_token_value, lengths,
    residual_in, o_weight, norm_gain, gate_logits, routes, w_gate, w_up, w_down,
):
    S, E = lax.axis_size("seq"), lax.axis_size("expert")
    R, D = residual_in.shape
    HEADS = query.shape[1] // HEAD_SIZE
    SPAN = cached_key_block.shape[1]
    KV = cached_key_block.shape[2]
    PIECES, _, FH = w_gate.shape
    N, T, W, HD = S * E, E * R, D // S, HEADS // S
    NA, NB = min(UP_SLOTS, PIECES * 4), min(DOWN_SLOTS, PIECES)
    vmem = pl.BlockSpec(memory_space=pltpu.VMEM)
    hbm = pl.BlockSpec(memory_space=pl.ANY)
    dma = pltpu.SemaphoreType.DMA
    read = 2 * (w_gate.size + w_up.size + w_down.size + o_weight.size + 2 * cached_key_block.size)
    return pl.pallas_call(
        functools.partial(layer_kernel, S, E, R, HEADS, D, FH, PIECES, NA, NB),
        out_shape=jax.ShapeDtypeStruct((R, W), BF),
        in_specs=[pl.BlockSpec(memory_space=pltpu.SMEM)] + [vmem] * 7 + [hbm] * 6,
        out_specs=vmem,
        scratch_shapes=[
            pltpu.VMEM((R, SPAN, KV), BF),
            pltpu.VMEM((R, SPAN, KV), BF),
            pltpu.VMEM(o_weight.shape, BF),
            pltpu.VMEM((NA, D // 2, FH), BF),
            pltpu.VMEM((NB, FH, D), BF),
            pltpu.VMEM((S, R + 1, HD, HEAD_SIZE), F32),
            pltpu.VMEM((S, R + 1, HD, HEAD_SIZE), F32),
            pltpu.VMEM((R, HD, HEAD_SIZE), F32),
            pltpu.VMEM((S, R, W), F32),
            pltpu.VMEM((S, R, W), F32),
            pltpu.VMEM((R, W), F32),
            pltpu.VMEM((R, W + 128), BF),
            pltpu.VMEM((S, E, R, W + 128), BF),
            pltpu.VMEM((2, T, D // 2), BF),
            pltpu.VMEM((S, T, W), F32),
            pltpu.VMEM((S, E, R, W), BF),
            pltpu.VMEM((N, R, W), BF),
            dma((2,)), dma((1,)), dma((NA,)), dma((NB,)),
            dma((S,)), dma((S,)), dma((S,)), dma((S,)),
            dma((N,)), dma((N,)), dma((N,)), dma((N,)),
        ],
        compiler_params=pltpu.CompilerParams(
            collective_id=0, has_side_effects=True, vmem_limit_bytes=60 * 1024 * 1024
        ),
        cost_estimate=pl.CostEstimate(flops=T * read, bytes_accessed=read, transcendentals=0),
    )(
        lengths, query.reshape(R, HEADS, HEAD_SIZE), fresh_token_key, fresh_token_value, residual_in,
        norm_gain.reshape(1, D), gate_logits, routes,
        cached_key_block, cached_value_block, o_weight, w_gate, w_up, w_down,
    )


def solution(mesh):
    placed = (
        P("expert", None),
        P("expert", "seq", None),
        P("expert", "seq", None),
        P("expert", None),
        P("expert", None),
        P("expert"),
        P("expert", None),
        P("seq", None),
        P(),
        P(),
        P(),
        P(("seq", "expert"), None, None),
        P(("seq", "expert"), None, None),
        P(("seq", "expert"), None, None),
    )
    return jax.shard_map(
        on_device, mesh=mesh, in_specs=placed, out_specs=P("expert", "seq"), check_vma=False
    )
```

time: 347 us -> 69.5 us (0.20)
  waiting for transfers between devices: 203 us -> 0 us
  blocking collectives: 70.3 us -> 0 us
  Pallas kernels: 0 us -> 63.1 us
  matrix products: 45.3 us -> 0 us
  between operations: 13.3 us -> 0.01 us
  other arithmetic: 8.75 us -> 0 us
    reduce_scatter x1 -> x0, waiting for transfers between devices: 133 us -> none  [on_device(): lax.psum_scatter(contrib, ('seq', 'expert'), scatter_dimension=0, tiled=T...]
    psum x1 -> x0, waiting for transfers between devices: 70.4 us -> none  [on_device(): projected = lax.psum(projected_part, 'seq')]
    all_gather x3 -> x0, blocking collectives: 70.3 us -> none  [the longest x2 63 us: combined_all(): pieces = jax.tree.map(lambda part: lax.all_gather(part, axis), value)]
    pallas_call x0 -> x1, Pallas kernels: none -> 63.1 us  [on_device(): pl.pallas_call(functools.partial(layer_kernel, S, E, R, HEADS, D, FH, PIE...]
    dot_general x11 -> x0, matrix products: 45.3 us -> none  [the longest x1 11.7 us: on_device(): jnp.einsum('npcf,pfd->npcd', hidden, w_down, preferred_element_type=jnp.f...]
    unnamed x8 -> x4, local copies, waits for them, and re-layouts: 0.41 us -> 5.57 us
  transfers between devices with their start and end apart: 3 -> 0, of which waited for: 2 -> 0; matrix products, arithmetic and copies ran while one was open for 2% -> 0% of each run, Pallas kernels for 0% -> 0%
where the time goes in v1:
time: 69.5 us; the launch traced here: 68.6 us
  Pallas kernels  63.1 us (91%)
  local copies, waits for them, and re-layouts  5.57 us (8%)
    pallas_call x1, Pallas kernels, on_device(): pl.pallas_call(functools.partial(layer_kernel, S, E, R, HEADS, D, FH, PIE...  63.1 us
    unnamed x4, local copies, waits for them, and re-layouts  5.57 us

profile of v1, /device:TPU:0, one launch (start us, length us, event | category | flops | bytes accessed | tf_op | source)
XLA Modules:
  0.0 68.6 jit_solution(6418515722536616615)
XLA Ops:
  0.0 1.4 %copy.15.logit_ref = f32[32,8]{1,0:T(8,128)} copy(f32[32,8]{0,1:T(8,128)} %param.23) | data formatting | bytes 2048 | tf_op args[9]
  1.4 1.4 %copy.16.route_ref = s32[32,8]{1,0:T(8,128)} copy(s32[32,8]{0,1:T(8,128)} %param.24) | data formatting | bytes 2048 | tf_op args[10]
  2.7 1.6 %copy.19 = bf16[1,8,64,128]{3,2,1,0:T(8,128)(2,1)} copy(bf16[1,8,64,128]{3,1,2,0:T(8,128)(2,1)} %bitcast.6) | data formatting | bytes 262144
  4.3 63.1 %shard_map.136 = bf16[8,512]{1,0:T(8,128)(2,1)} custom-call(s32[8]{0:T(128)} %len_ref.1, bf16[8,64,128]{2,1,0:T(8,128)(2,1)} %bitcast.5, bf16[8,512]{1,0:T(8,128)(2,1)} %fk_ref.1, bf16[8,512]{1,0:T(8,128)(2,1)} %fv_ref.1, bf16[8,4096]{1,0:T(8,128)(2,1)} %res_ref.1, f32[1,4096]{1,0:T(1,128)} %bitcast.7, f32[32,8]{1,0:T(8,128)} %copy.15.logit_ref, ...), custom_call_target="tpu_custom_call" | custom-call | flops 2751463424 | bytes 85983232 | tf_op jit(solution)/shard_map/pallas_call | solution.py:342
  67.3 1.3 %copy.21 = bf16[8,512]{1,0:T(8,128)(2,1)} copy(bf16[8,512]{1,0:T(8,128)(2,1)} %shard_map.136) | data formatting | bytes 16384

commit v2 on v1

--- a/solution.py
+++ b/solution.py
@@ -11,10 +11,17 @@
 KEY_VALUE_HEADS = 4
 HEAD_SIZE = 128
 MESH = pl.DeviceIdType.MESH
-UP_SLOTS = 8
+CAP = 2
+UP_SLOTS = 12
 DOWN_SLOTS = 2
 BF = jnp.bfloat16
 F32 = jnp.float32
+
+
+def split3(value):
+    first = value.astype(BF).astype(F32)
+    second = (value - first).astype(BF).astype(F32)
+    return [first, second, (value - first - second).astype(BF).astype(F32)]
 
 
 def layer_kernel(
@@ -23,12 +30,16 @@
     k_hbm, v_hbm, ow_hbm, wg_hbm, wu_hbm, wd_hbm,
     out_ref,
     kbuf, vbuf, owbuf, abuf, bbuf,
-    sbuf1, rbuf1, att, sbuf2, rbuf2, strm, xsend, xg, xs, acc, cbuf, rc,
+    qbuf, sbuf1, rbuf1, att, sbuf2, rbuf2, strm, xsend, xg, xs, acc, cbuf, rc,
     kv_sem, ow_sem, a_sem, b_sem,
     ss1, rs1, ss2, rs2, ss3, rs3, ss4, rs4,
 ):
     N = S * E
     T = E * R
+    LOCAL = max(1, PIECES // 2)
+    L = LOCAL * CAP
+    M = E * L
+    NL = N * L
     W = D // S
     HD = HEADS // S
     KVH = KEY_VALUE_HEADS
@@ -37,6 +48,7 @@
     SPAN = kbuf.shape[1]
     HALF = D // 2
     TA = PIECES * 4
+    REUSE = PIECES > NB and owbuf.shape[0] >= FH
     seq = lax.axis_index("seq")
     exp = lax.axis_index("expert")
     me = seq * E + exp
@@ -83,15 +95,22 @@
     lane = lax.broadcasted_iota(jnp.int32, (HEADS, HS), 1)
     has_own = seq == 0
 
+    def joined(parts, i, r):
+        cut = [parts[:, :, (i + k) * R + r : (i + k) * R + r + 1] for k in range(3)]
+        return cut[0] + cut[1] + cut[2]
+
     def spread(row):
         return jnp.concatenate(
             [jnp.broadcast_to(row[:, k * HS : (k + 1) * HS], (GROUP, HS)) for k in range(KVH)], axis=0
         )
 
+    for h in range(HEADS):
+        qbuf[h] = q_ref[:, h * HS : (h + 1) * HS].astype(F32)
+    queries = [qbuf[:, r, :] for r in range(R)]
     k_copy.wait()
     scores = []
     for r in range(R):
-        q = q_ref[r]
+        q = queries[r].astype(BF)
         wide = jnp.where(diag, jnp.concatenate([q] * KVH, axis=1), jnp.zeros((), BF))
         scores.append(
             lax.dot_general(wide, kbuf[r], (((1,), (1,)), ((), ())), preferred_element_type=F32) * scale
@@ -103,7 +122,7 @@
     for r in range(R):
         valid = position < len_ref[r]
         masked = jnp.where(valid, scores[r], -1e30)
-        own = jnp.sum(q_ref[r].astype(F32) * spread(fk[r : r + 1]), axis=1, keepdims=True) * scale
+        own = jnp.sum(queries[r] * spread(fk[r : r + 1]), axis=1, keepdims=True) * scale
         own = jnp.where(has_own, own, -1e30)
         peak = jnp.maximum(jnp.max(masked, axis=1, keepdims=True), own)
         weight = jnp.where(valid, jnp.exp(masked - peak), 0.0)
@@ -117,11 +136,34 @@
             [both[k * GROUP : (k + 1) * GROUP, k * HS : (k + 1) * HS] for k in range(KVH)], axis=0
         )
         summed = summed + own_weight * spread(fv[r : r + 1])
-        packed = jnp.where(lane == r, peak, jnp.where(lane == R + r, total, packed))
+        for i, part in enumerate(split3(peak) + split3(total)):
+            packed = jnp.where(lane == i * R + r, part, packed)
         for s in range(S):
-            sbuf1[s, r] = summed[s * HD : (s + 1) * HD]
+            sbuf1[s, r] = summed[s * HD : (s + 1) * HD].astype(BF)
     for s in range(S):
-        sbuf1[s, R] = packed[s * HD : (s + 1) * HD]
+        sbuf1[s, R] = packed[s * HD : (s + 1) * HD].astype(BF)
+
+    logits = logit_ref[...]
+    odds = jnp.exp(logits - jnp.max(logits, axis=0, keepdims=True))
+    gates = odds / jnp.sum(odds, axis=0, keepdims=True)
+    routes = route_ref[...]
+    slot_id = lax.broadcasted_iota(jnp.int32, (NL, T), 0)
+    place = slot_id % L
+    slot_expert = ((slot_id // L) * PIECES) // 2 + place // CAP
+    row_id = lax.broadcasted_iota(jnp.int32, (NL, T), 1)
+    hits = jnp.zeros((NL, T), F32)
+    share = jnp.zeros((NL, T), F32)
+    for k in range(routes.shape[0]):
+        match = (routes[k : k + 1] == slot_expert) & (row_id // R == exp)
+        hits = jnp.where(match, 1.0, hits)
+        share = share + jnp.where(match, gates[k : k + 1], 0.0)
+    earlier = lax.broadcasted_iota(jnp.int32, (T, T), 0) < lax.broadcasted_iota(jnp.int32, (T, T), 1)
+    before = jnp.dot(
+        hits.astype(BF), jnp.where(earlier, 1.0, 0.0).astype(BF), preferred_element_type=F32
+    )
+    taken = (hits > 0.5) & (before == (place % CAP).astype(F32))
+    chosen = jnp.where(taken, 1.0, 0.0)
+    share = jnp.where(taken, share, 0.0)
 
     pl.semaphore_wait(barrier, N - 1)
 
@@ -144,12 +186,12 @@
     rbuf1[0] = sbuf1[seq]
     lax.fori_loop(1, S, wait1, 0)
 
-    stats = rbuf1[:, R]
+    stats = rbuf1[:, R].astype(F32)
     for r in range(R):
-        peak = stats[:, :, r : r + 1]
-        total = stats[:, :, R + r : R + r + 1]
+        peak = joined(stats, 0, r)
+        total = joined(stats, 3, r)
         factor = jnp.exp(peak - jnp.max(peak, axis=0, keepdims=True))
-        att[r] = jnp.sum(factor * rbuf1[:, r], axis=0) / jnp.sum(factor * total, axis=0)
+        att[r] = jnp.sum(factor * rbuf1[:, r].astype(F32), axis=0) / jnp.sum(factor * total, axis=0)
     attended = jnp.concatenate([att[:, h, :] for h in range(HD)], axis=1).astype(BF)
 
     ow_copy.wait()
@@ -166,7 +208,7 @@
         return jnp.dot(attended, owbuf[:, cols], preferred_element_type=F32)
 
     def start2(j, _):
-        sbuf2[j] = project(j)
+        sbuf2[j] = project(j).astype(BF)
         copy2(j).start()
         return 0
 
@@ -175,21 +217,27 @@
         return 0
 
     lax.fori_loop(1, S, start2, 0)
-    rbuf2[0] = project(0)
+    own_projected = project(0)
+    rbuf2[0] = jnp.zeros((R, W), BF)
+    if REUSE:
+        pltpu.make_async_copy(wd_hbm.at[NB], owbuf.at[pl.ds(0, FH), :], b_sem.at[NB]).start()
     lax.fori_loop(1, S, wait2, 0)
 
     own_cols = pl.ds(pl.multiple_of(seq * W, W), W)
-    stream = res_ref[:, own_cols].astype(F32) + jnp.sum(rbuf2[...], axis=0)
+    stream = res_ref[:, own_cols].astype(F32) + own_projected + jnp.sum(rbuf2[...].astype(F32), axis=0)
     strm[...] = stream
     squares = jnp.sum(stream * stream, axis=1, keepdims=True)
-    part0 = squares.astype(BF).astype(F32)
-    part1 = (squares - part0).astype(BF).astype(F32)
-    part2 = squares - part0 - part1
+    parts = split3(squares)
     lane_r = lax.broadcasted_iota(jnp.int32, (R, 128), 1)
-    tail = jnp.where(
-        lane_r == 0, part0, jnp.where(lane_r == 1, part1, jnp.where(lane_r == 2, part2, 0.0))
+    tail = jnp.zeros((R, 128), F32)
+    for i in range(3):
+        tail = jnp.where(lane_r == i, parts[i], tail)
+    sent = jnp.concatenate([stream * gain_ref[:, own_cols], tail], axis=1)
+    slots = jnp.dot(
+        chosen.astype(BF), jnp.concatenate([sent] * E, axis=0).astype(BF), preferred_element_type=F32
     )
-    xsend[...] = jnp.concatenate([stream * gain_ref[:, own_cols], tail], axis=1).astype(BF)
+    for t in range(N):
+        xsend[t] = slots[t * L : (t + 1) * L].astype(BF)
 
     def target(j):
         t = lax.rem(me + j, N)
@@ -198,7 +246,7 @@
     def copy3(j, dst):
         ts, te = target(j)
         return pltpu.make_async_remote_copy(
-            src_ref=xsend, dst_ref=dst, send_sem=ss3.at[j], recv_sem=rs3.at[j],
+            src_ref=xsend.at[ts * E + te], dst_ref=dst, send_sem=ss3.at[j], recv_sem=rs3.at[j],
             device_id={"seq": ts, "expert": te}, device_id_type=MESH,
         )
 
@@ -212,16 +260,12 @@
         return 0
 
     lax.fori_loop(1, N, start3, 0)
-    xg[seq, exp] = xsend[...]
-
-    logits = logit_ref[...]
-    odds = jnp.exp(logits - jnp.max(logits, axis=1, keepdims=True))
-    gates = odds / jnp.sum(odds, axis=1, keepdims=True)
+    xg[seq, exp] = xsend[me]
 
     lax.fori_loop(1, N, wait3, 0)
-    squares = jnp.zeros((T, 1), F32)
+    squares = jnp.zeros((M, 1), F32)
     for s in range(S):
-        block = xg[s].astype(F32).reshape(T, W + 128)
+        block = jnp.concatenate([xg[s, e].astype(F32) for e in range(E)], axis=0)
         xs[(s * W) // HALF, :, (s * W) % HALF : (s * W) % HALF + W] = block[:, :W].astype(BF)
         squares = squares + jnp.sum(block[:, W:], axis=1, keepdims=True)
     inverse = lax.rsqrt(squares * (1.0 / D) + 1e-6)
@@ -240,7 +284,11 @@
                 unit = p * 4 + i
                 slot = lax.rem(unit, NA)
                 a_copy(p, i, slot).wait()
-                part = jnp.dot(xs[half], abuf[slot], preferred_element_type=F32)
+                part = jnp.zeros((M, FH), F32)
+                for k in range(0, HALF, 512):
+                    part = part + jnp.dot(
+                        xs[half, :, k : k + 512], abuf[slot, k : k + 512, :], preferred_element_type=F32
+                    )
                 if half == 0:
                     acts.append(part)
                 else:
@@ -254,43 +302,56 @@
         gate_act = acts[0] * inverse
         up_act = acts[1] * inverse
         hidden = (gate_act / (1.0 + jnp.exp(-gate_act)) * up_act).astype(BF)
-        expert_id = (me * PIECES + p) // 2
-        coeff = jnp.sum(jnp.where(route_ref[...] == expert_id, gates, 0.0), axis=1, keepdims=True)
-        slot = lax.rem(p, NB)
-        b_copy(p, slot).wait()
-
-        def columns(j, _):
-            c = lax.rem(seq + j, S)
-            cols = pl.ds(pl.multiple_of(c * W, W), W)
-            result = coeff * jnp.dot(hidden, bbuf[slot, :, cols], preferred_element_type=F32)
-
-            @pl.when(p == 0)
+        local = (lax.broadcasted_iota(jnp.int32, (M, W), 0) % L) // CAP == p // 2
+        def combine(view):
+            def columns(j, _):
+                c = lax.rem(seq + j, S)
+                cols = pl.ds(pl.multiple_of(c * W, W), W)
+                result = jnp.dot(hidden, view[pl.ds(0, FH), cols], preferred_element_type=F32)
+                result = jnp.where(local, result, 0.0)
+
+                @pl.when(p == 0)
+                def _():
+                    acc[c] = result
+
+                @pl.when(p > 0)
+                def _():
+                    acc[c] = acc[c] + result
+
+                @pl.when(p == PIECES - 1)
+                def _():
+                    value = acc[c]
+                    for e in range(E):
+                        cbuf[c, e] = value[e * L : (e + 1) * L].astype(BF)
+
+                        @pl.when(c * E + e != me)
+                        def _():
+                            copy4(c, e).start()
+
+                return 0
+
+            lax.fori_loop(1, S + 1, columns, 0)
+
+        slot = lax.rem(p - p // (NB + 1), NB)
+        if REUSE:
+
+            @pl.when(p == NB)
             def _():
-                acc[c] = result
-
-            @pl.when(p > 0)
+                pltpu.make_async_copy(wd_hbm.at[p], owbuf.at[pl.ds(0, FH), :], b_sem.at[NB]).wait()
+                combine(owbuf)
+
+            @pl.when(p != NB)
             def _():
-                acc[c] = acc[c] + result
-
-            @pl.when(p == PIECES - 1)
+                b_copy(p, slot).wait()
+                combine(bbuf.at[slot])
+
+            @pl.when((p < NB) & (p + NB + 1 < PIECES))
             def _():
-                value = acc[c]
-                for e in range(E):
-                    cbuf[c, e] = value[e * R : (e + 1) * R].astype(BF)
-
-                    @pl.when(c * E + e != me)
-                    def _():
-                        copy4(c, e).start()
-
-            return 0
-
-        lax.fori_loop(1, S + 1, columns, 0)
-        if PIECES > NB:
-
-            @pl.when(p + NB < PIECES)
-            def _():
-                b_copy(p + NB, slot).start()
-
+                b_copy(p + NB + 1, slot).start()
+
+        else:
+            b_copy(p, slot).wait()
+            combine(bbuf.at[slot])
         return 0
 
     lax.fori_loop(0, PIECES, piece, 0)
@@ -306,7 +367,16 @@
         return 0
 
     lax.fori_loop(1, N, wait4, 0)
-    out_ref[...] = (strm[...] + jnp.sum(rc[...].astype(F32), axis=0)).astype(BF)
+    back = jnp.concatenate([rc[t].astype(F32) for t in range(N)], axis=0).astype(BF)
+    share_high = share.astype(BF)
+    share_low = (share - share_high.astype(F32)).astype(BF)
+    turned = (((0,), (0,)), ((), ()))
+    added = lax.dot_general(share_high, back, turned, preferred_element_type=F32)
+    added = added + lax.dot_general(share_low, back, turned, preferred_element_type=F32)
+    total = strm[...]
+    for e in range(E):
+        total = total + added[e * R : (e + 1) * R]
+    out_ref[...] = total.astype(BF)
 
     def sent12(j, _):
         copy1(j).wait_send()
@@ -334,7 +404,10 @@
     KV = cached_key_block.shape[2]
     PIECES, _, FH = w_gate.shape
     N, T, W, HD = S * E, E * R, D // S, HEADS // S
+    L = max(1, PIECES // 2) * CAP
+    M = E * L
     NA, NB = min(UP_SLOTS, PIECES * 4), min(DOWN_SLOTS, PIECES)
+    assert PIECES <= 4 and (PIECES <= NB or o_weight.shape[0] >= FH)
     vmem = pl.BlockSpec(memory_space=pltpu.VMEM)
     hbm = pl.BlockSpec(memory_space=pl.ANY)
     dma = pltpu.SemaphoreType.DMA
@@ -350,29 +423,30 @@
             pltpu.VMEM(o_weight.shape, BF),
             pltpu.VMEM((NA, D // 2, FH), BF),
             pltpu.VMEM((NB, FH, D), BF),
-            pltpu.VMEM((S, R + 1, HD, HEAD_SIZE), F32),
-            pltpu.VMEM((S, R + 1, HD, HEAD_SIZE), F32),
+            pltpu.VMEM((HEADS, R, HEAD_SIZE), F32),
+            pltpu.VMEM((S, R + 1, HD, HEAD_SIZE), BF),
+            pltpu.VMEM((S, R + 1, HD, HEAD_SIZE), BF),
             pltpu.VMEM((R, HD, HEAD_SIZE), F32),
-            pltpu.VMEM((S, R, W), F32),
-            pltpu.VMEM((S, R, W), F32),
+            pltpu.VMEM((S, R, W), BF),
+            pltpu.VMEM((S, R, W), BF),
             pltpu.VMEM((R, W), F32),
-            pltpu.VMEM((R, W + 128), BF),
-            pltpu.VMEM((S, E, R, W + 128), BF),
-            pltpu.VMEM((2, T, D // 2), BF),
-            pltpu.VMEM((S, T, W), F32),
-            pltpu.VMEM((S, E, R, W), BF),
-            pltpu.VMEM((N, R, W), BF),
-            dma((2,)), dma((1,)), dma((NA,)), dma((NB,)),
+            pltpu.VMEM((N, L, W + 128), BF),
+            pltpu.VMEM((S, E, L, W + 128), BF),
+            pltpu.VMEM((2, M, D // 2), BF),
+            pltpu.VMEM((S, M, W), F32),
+            pltpu.VMEM((S, E, L, W), BF),
+            pltpu.VMEM((N, L, W), BF),
+            dma((2,)), dma((1,)), dma((NA,)), dma((NB + 1,)),
             dma((S,)), dma((S,)), dma((S,)), dma((S,)),
             dma((N,)), dma((N,)), dma((N,)), dma((N,)),
         ],
         compiler_params=pltpu.CompilerParams(
-            collective_id=0, has_side_effects=True, vmem_limit_bytes=60 * 1024 * 1024
+            collective_id=0, has_side_effects=True, vmem_limit_bytes=63 * 1024 * 1024
         ),
         cost_estimate=pl.CostEstimate(flops=T * read, bytes_accessed=read, transcendentals=0),
     )(
-        lengths, query.reshape(R, HEADS, HEAD_SIZE), fresh_token_key, fresh_token_value, residual_in,
-        norm_gain.reshape(1, D), gate_logits, routes,
+        lengths, query, fresh_token_key, fresh_token_value, residual_in,
+        norm_gain.reshape(1, D), gate_logits.T, routes.T,
         cached_key_block, cached_value_block, o_weight, w_gate, w_up, w_down,
     )
 

time: 69.5 us -> 62.1 us (0.89)
  local copies, waits for them, and re-layouts: 5.57 us -> 1.3 us
  Pallas kernels: 63.1 us -> 60.6 us
    unnamed x4 -> x1, local copies, waits for them, and re-layouts: 5.57 us -> 1.3 us
    pallas_call x1, Pallas kernels: 63.1 us -> 60.6 us  [on_device(): pl.pallas_call(functools.partial(layer_kernel, S, E, R, HEADS, D, FH, PIE...]
where the time goes in v2:
time: 62.1 us; the launch traced here: 61.9 us
  Pallas kernels  60.6 us (98%)
  local copies, waits for them, and re-layouts  1.3 us (2%)
    pallas_call x1, Pallas kernels, on_device(): pl.pallas_call(functools.partial(layer_kernel, S, E, R, HEADS, D, FH, PIE...  60.6 us
    unnamed x1, local copies, waits for them, and re-layouts  1.3 us

profile of v2, /device:TPU:0, one launch (start us, length us, event | category | flops | bytes accessed | tf_op | source)
XLA Modules:
  0.0 61.9 jit_solution(1434834655040586771)
XLA Ops:
  0.0 60.6 %shard_map.136 = bf16[8,512]{1,0:T(8,128)(2,1)} custom-call(s32[8]{0:T(128)} %len_ref.1, bf16[8,8192]{1,0:T(8,128)(2,1)} %q_ref.1, bf16[8,512]{1,0:T(8,128)(2,1)} %fk_ref.1, bf16[8,512]{1,0:T(8,128)(2,1)} %fv_ref.1, bf16[8,4096]{1,0:T(8,128)(2,1)} %res_ref.1, f32[1,4096]{1,0:T(1,128)} %bitcast.3, f32[8,32]{1,0:T(8,128)} %bitcast.4, s32[8,32]{1,0:T(8,128)} %bitcast.5, ...), custom_call_target="tpu_custom_call" | custom-call | flops 2751463424 | bytes 85983232 | tf_op jit(solution)/shard_map/pallas_call | solution.py:415
  60.6 1.3 %copy.16 = bf16[8,512]{1,0:T(8,128)(2,1)} copy(bf16[8,512]{1,0:T(8,128)(2,1)} %shard_map.136) | data formatting | bytes 16384

commit v3 on v2

--- a/solution.py
+++ b/solution.py
@@ -12,7 +12,7 @@
 HEAD_SIZE = 128
 MESH = pl.DeviceIdType.MESH
 CAP = 2
-UP_SLOTS = 12
+UP_SLOTS = 8
 DOWN_SLOTS = 2
 BF = jnp.bfloat16
 F32 = jnp.float32
@@ -62,7 +62,6 @@
         )
         return 0
 
-    lax.fori_loop(1, N, greet, 0)
 
     k_copy = pltpu.make_async_copy(k_hbm, kbuf, kv_sem.at[0])
     v_copy = pltpu.make_async_copy(v_hbm, vbuf, kv_sem.at[1])
@@ -86,6 +85,8 @@
                 a_copy(p, i, p * 4 + i).start()
         if p < NB:
             b_copy(p, p).start()
+
+    lax.fori_loop(1, N, greet, 0)
 
     scale = 1.0 / math.sqrt(HS)
     head_row = lax.broadcasted_iota(jnp.int32, (HEADS, KVH * HS), 0) // GROUP
@@ -285,9 +286,9 @@
                 slot = lax.rem(unit, NA)
                 a_copy(p, i, slot).wait()
                 part = jnp.zeros((M, FH), F32)
-                for k in range(0, HALF, 512):
+                for k in range(0, HALF, HALF):
                     part = part + jnp.dot(
-                        xs[half, :, k : k + 512], abuf[slot, k : k + 512, :], preferred_element_type=F32
+                        xs[half, :, k : k + HALF], abuf[slot, k : k + HALF, :], preferred_element_type=F32
                     )
                 if half == 0:
                     acts.append(part)

time: 62.1 us -> 56.9 us (0.916)
  Pallas kernels: 60.6 us -> 55.4 us
    pallas_call x1, Pallas kernels: 60.6 us -> 55.4 us  [on_device(): pl.pallas_call(functools.partial(layer_kernel, S, E, R, HEADS, D, FH, PIE...]
where the time goes in v3:
time: 56.9 us; the launch traced here: 56.7 us
  Pallas kernels  55.4 us (97%)
  local copies, waits for them, and re-layouts  1.3 us (2%)
    pallas_call x1, Pallas kernels, on_device(): pl.pallas_call(functools.partial(layer_kernel, S, E, R, HEADS, D, FH, PIE...  55.4 us
    unnamed x1, local copies, waits for them, and re-layouts  1.3 us

profile of v3, /device:TPU:0, one launch (start us, length us, event | category | flops | bytes accessed | tf_op | source)
XLA Modules:
  0.0 56.7 jit_solution(9477883254292553545)
XLA Ops:
  0.0 55.4 %shard_map.136 = bf16[8,512]{1,0:T(8,128)(2,1)} custom-call(s32[8]{0:T(128)} %len_ref.1, bf16[8,8192]{1,0:T(8,128)(2,1)} %q_ref.1, bf16[8,512]{1,0:T(8,128)(2,1)} %fk_ref.1, bf16[8,512]{1,0:T(8,128)(2,1)} %fv_ref.1, bf16[8,4096]{1,0:T(8,128)(2,1)} %res_ref.1, f32[1,4096]{1,0:T(1,128)} %bitcast.3, f32[8,32]{1,0:T(8,128)} %bitcast.4, s32[8,32]{1,0:T(8,128)} %bitcast.5, ...), custom_call_target="tpu_custom_call" | custom-call | flops 2751463424 | bytes 85983232 | tf_op jit(solution)/shard_map/pallas_call | solution.py:416
  55.4 1.3 %copy.16 = bf16[8,512]{1,0:T(8,128)(2,1)} copy(bf16[8,512]{1,0:T(8,128)(2,1)} %shard_map.136) | data formatting | bytes 16384
